TPU v7x, 128 devices: a whole 4x4x4 slice. The times are simulated.
128 devices in a mesh: dp: 4 (over x), block: 32 (over z, y, core).
Axes of the slice: x: 4, y: 4, z: 4, core: 2. Of those that a mesh axis runs over, the one named last changes fastest.
Arguments:
- grad: float32 [1024, 28672], P(('dp', 'block')), may hold values from -6 to 6
- factors: float32 [4, 32, 1024, 1024], P('dp', 'block'), as said below
- owners: int32 [28], replicated, may hold values from 0 to 31, as said below
Outputs:
- new_factors: float32 [4, 32, 1024, 1024], P('dp', 'block')
- update: float32 [1024, 28672], P(('dp', 'block'))
Inputs may be any that keep to these rules, and one draw needn't show every extreme that they name: `owners`: no owner is named more than 2 times, and some owner exactly 2 times. `factors`: every [1024, 1024] matrix is symmetric positive definite.
All inputs are finite; a program needn't handle non-finite values.
Results may differ from a plain program's by a relative error of at most 0.00013.
Values sent between devices are 32-bit elements; how exact they have to be, the bound alone decides.
No kernel may reach another device: no remote copies, remote signals or barrier semaphores. Data moves between devices by JAX's collectives and lax.ppermute only.
A program may use at most 128 MiB of HBM per device.

v0:
```python
import jax
import jax.numpy as jnp
from jax import lax
from jax.experimental import pallas as pl
from jax.experimental.pallas import tpu as pltpu
from jax.sharding import PartitionSpec as P

BOTH = ("dp", "block")
TILE = 256
OUTER_ORDER = (0, 3, 1, 2)
INNER_ORDER = (1, 2, 0, 3)
MIB = 1024 * 1024

decay_rate = 0.9
epsilon = 1e-06


def vmem():
    return pl.BlockSpec(memory_space=pltpu.VMEM)


def anywhere():
    return pl.BlockSpec(memory_space=pl.ANY)


def resident(x):
    return pltpu.with_memory_space_constraint(x, pltpu.VMEM)


def in_hbm(x):
    return pltpu.with_memory_space_constraint(x, pltpu.HBM)


def smem():
    return pl.BlockSpec(memory_space=pltpu.SMEM)


def diag_mask():
    rows = lax.broadcasted_iota(jnp.int32, (TILE, TILE), 0)
    cols = lax.broadcasted_iota(jnp.int32, (TILE, TILE), 1)
    return rows, cols


def span(index):
    return slice(index * TILE, (index + 1) * TILE)


def split(value):
    high = value.astype(jnp.bfloat16)
    low = (value - high.astype(jnp.float32)).astype(jnp.bfloat16)
    return high, low


def dot3(a_high, a_low, b_high, b_low):
    def one(a, b):
        return jnp.dot(a, b, preferred_element_type=jnp.float32)

    return one(a_high, b_high) + (one(a_high, b_low) + one(a_low, b_high))


def put_split(high_ref, low_ref, i, j, block):
    high, low = split(block)
    high_ref[span(i), span(j)] = high
    low_ref[span(i), span(j)] = low


def put_both(high_ref, low_ref, i, j, block):
    put_split(high_ref, low_ref, i, j, block)
    if i != j:
        put_split(high_ref, low_ref, j, i, block.T)


def place_of(owners_ref, count_ref, c):
    owner = owners_ref[c]
    slot = count_ref[owner]
    count_ref[owner] = slot + 1
    return slot * count_ref.shape[0] + owner


def clear(count_ref):
    @pl.loop(0, count_ref.shape[0])
    def _(o):
        count_ref[o] = 0


def deal_kernel(owners_ref, grad_hbm, out_hbm, count_ref, buffer, load_sem, sem):
    load = pltpu.make_async_copy(grad_hbm, buffer, load_sem)
    load.start()
    clear(count_ref)
    load.wait()
    deal_blocks(owners_ref, buffer, out_hbm, count_ref, sem)


def deal_resident_kernel(owners_ref, grad, out_hbm, count_ref, sem):
    clear(count_ref)
    deal_blocks(owners_ref, grad, out_hbm, count_ref, sem)


def deal_blocks(owners_ref, grad, out_hbm, count_ref, sem):
    width = out_hbm.shape[-1]
    for c in range(owners_ref.shape[0]):
        place = place_of(owners_ref, count_ref, c)
        cols = slice(c * width, (c + 1) * width)
        pltpu.make_async_copy(grad.at[:, cols], out_hbm.at[place], sem).start()
    pltpu.make_async_copy(grad, grad, sem).wait()


def collect_kernel(owners_ref, back, out_hbm, count_ref, sem):
    width = back.shape[-1]
    clear(count_ref)
    for c in range(owners_ref.shape[0]):
        place = place_of(owners_ref, count_ref, c)
        cols = slice(c * width, (c + 1) * width)
        pltpu.make_async_copy(back.at[place], out_hbm.at[:, cols], sem).start()
    pltpu.make_async_copy(out_hbm, out_hbm, sem).wait()


def deal(owners, grad, owner_count, landed):
    rows = grad.shape[0]
    count = owners.shape[0]
    width = grad.shape[1] // count
    counts, sem = pltpu.SMEM((owner_count,), jnp.int32), pltpu.SemaphoreType.DMA(())
    buffers = [pltpu.VMEM(grad.shape, jnp.float32), sem, sem]
    return pl.pallas_call(
        deal_resident_kernel if landed else deal_kernel,
        out_shape=pltpu.HBM((2 * owner_count, rows, width), jnp.float32),
        in_specs=[smem(), vmem() if landed else anywhere()],
        out_specs=anywhere(),
        scratch_shapes=[counts, sem] if landed else [counts] + buffers,
        compiler_params=pltpu.CompilerParams(vmem_limit_bytes=16 * MIB),
        cost_estimate=pl.CostEstimate(flops=5 * 10**10, bytes_accessed=2**22, transcendentals=0),
        name="deal",
    )(owners, resident(grad) if landed else in_hbm(grad))


def collect(owners, back):
    places, rows, width = back.shape
    return pl.pallas_call(
        collect_kernel,
        out_shape=jax.ShapeDtypeStruct((rows, owners.shape[0] * width), jnp.float32),
        in_specs=[smem(), vmem()],
        out_specs=anywhere(),
        scratch_shapes=[
            pltpu.SMEM((places // 2,), jnp.int32),
            pltpu.SemaphoreType.DMA(()),
        ],
        compiler_params=pltpu.CompilerParams(vmem_limit_bytes=16 * MIB),
        cost_estimate=pl.CostEstimate(flops=0, bytes_accessed=2**22, transcendentals=0),
        name="collect",
    )(owners, resident(back))


def lower_blocks(tiles):
    return [(i, j) for j in range(tiles) for i in range(j + 1, tiles)]


def root_kernel(
    a_hbm, xh_hbm, xl_hbm, pack_hbm,
    a, sh, sl, s2, s2h, s2l, s3h, s3l, qh, ql, xh, xl, pack, in_sems, out_sems,
):
    size = a.shape[0]
    tiles = size // TILE
    rows, cols = diag_mask()
    on_diag = rows == cols
    loads = [
        pltpu.make_async_copy(a_hbm.at[span(b)], a.at[span(b)], in_sems.at[b]) for b in range(tiles)
    ]
    for load in loads:
        load.start()
    diagonal = jnp.zeros((8, TILE), jnp.float32)
    for b in range(tiles):
        loads[b].wait()
        block = jnp.where(on_diag, a[span(b), span(b)], 0.0)
        diagonal += jnp.sum(block.reshape(TILE // 8, 8, TILE), axis=0)
    shrink = 0.25 / (2.0 * jnp.sum(diagonal) / size)

    def step_block(i, j):
        block = a[span(i), span(j)] * -shrink
        if i == j:
            block = jnp.where(on_diag, 1.25 + block, block)
        return block

    for i in range(tiles):
        for j in range(tiles):
            put_split(sh, sl, i, j, step_block(i, j))

    def product(ah, al, bh, bl, j):
        low_rows = slice(j * TILE, size)
        return dot3(ah[low_rows, :], al[low_rows, :], bh[:, span(j)], bl[:, span(j)])

    for j in range(tiles):
        column = product(sh, sl, sh, sl, j)
        s2[j * TILE :, span(j)] = column
        for i in range(j, tiles):
            put_both(s2h, s2l, i, j, column[span(i - j)])
    for j in range(tiles):
        column = product(sh, sl, s2h, s2l, j)
        for i in range(j, tiles):
            block = column[span(i - j)]
            put_both(s3h, s3l, i, j, block)
            put_both(qh, ql, i, j, block - 1.25 * s2[span(i), span(j)])

    stores = []

    def store(source, target, where):
        k = len(stores)
        stores.append(pltpu.make_async_copy(source.at[where], target.at[where], out_sems.at[k]))
        stores[-1].start()

    offset = len(lower_blocks(tiles))
    last = (offset + tiles // 2) * TILE
    for j in range(tiles):
        column = product(s3h, s3l, qh, ql, j)
        for i in range(j, tiles):
            block = column[span(i - j)] + 1.25 * step_block(i, j)
            put_both(xh, xl, i, j, block)
            if i != j:
                pack[span(lower_blocks(tiles).index((i, j)))] = block
            else:
                s2[span(i), span(i)] = block
        if j + 1 < tiles:
            first = lower_blocks(tiles).index((j + 1, j))
            store(pack, pack_hbm, slice(first * TILE, (first + tiles - 1 - j) * TILE))
        if j % 2:
            first, second = s2[span(j - 1), span(j - 1)], s2[span(j), span(j)]
            pack[span(offset + j // 2)] = jnp.where(rows >= cols, first, second)
            line = jnp.sum(jnp.where(on_diag, second, 0.0), axis=0, keepdims=True)
            start = last + j // 2 * 8
            pack[start : start + 8] = jnp.broadcast_to(line, (8, TILE))
            store(pack, pack_hbm, span(offset + j // 2))
            store(pack, pack_hbm, slice(start, start + 8))
        store(xh, xh_hbm, span(j))
        store(xl, xl_hbm, span(j))
    for copy in stores:
        copy.wait()


def packed_rows(size):
    tiles = size // TILE
    return (len(lower_blocks(tiles)) + tiles // 2) * TILE + 8 * (tiles // 2)


def root(factor):
    size = factor.shape[0]
    tiles = size // TILE
    half = pltpu.HBM((size, size), jnp.bfloat16)
    square = pltpu.VMEM((size, size), jnp.float32)
    square_half = pltpu.VMEM((size, size), jnp.bfloat16)
    packed = (packed_rows(size), TILE)
    return pl.pallas_call(
        root_kernel,
        out_shape=[half, half, pltpu.HBM(packed, jnp.float32)],
        in_specs=[anywhere()],
        out_specs=[anywhere()] * 3,
        scratch_shapes=[square, square_half, square_half, square]
        + [square_half] * 8
        + [
            pltpu.VMEM(packed, jnp.float32),
            pltpu.SemaphoreType.DMA((tiles,)),
            pltpu.SemaphoreType.DMA((4 * tiles - 1,)),
        ],
        compiler_params=pltpu.CompilerParams(vmem_limit_bytes=44 * MIB),
        cost_estimate=pl.CostEstimate(flops=0, bytes_accessed=0, transcendentals=0),
        name="root",
    )(in_hbm(factor))


def unpack_block(pack_ref, tiles, i, j, rows, cols):
    if i != j:
        return pack_ref[span(lower_blocks(tiles).index((i, j)))]
    offset = len(lower_blocks(tiles))
    last = (offset + tiles // 2) * TILE
    both = pack_ref[span(offset + i // 2)]
    if i % 2 == 0:
        return jnp.where(rows >= cols, both, both.T)
    diagonal = pack_ref[last + (i // 2) * 8 : last + (i // 2) * 8 + 1]
    return jnp.where(rows == cols, diagonal, jnp.where(rows < cols, both, both.T))


def unpack_column(pack_ref, tiles, j, high_ref, low_ref):
    rows, cols = diag_mask()
    for i in range(j, tiles):
        put_both(high_ref, low_ref, i, j, unpack_block(pack_ref, tiles, i, j, rows, cols))


def unpack_left(place_ref, pack_ref, tiles, parts, high_ref, low_ref):
    rows, cols = diag_mask()

    def by_order(order):
        for r in range(tiles // 2):
            for c in range(*parts):
                i, j = order[r], order[c]
                block = unpack_block(pack_ref, tiles, max(i, j), min(i, j), rows, cols)
                put_split(high_ref, low_ref, r, c - parts[0], block if i >= j else block.T)

    pl.when(place_ref[1] == 0)(lambda: by_order(OUTER_ORDER))
    pl.when(place_ref[1] != 0)(lambda: by_order(INNER_ORDER))


def squares(block):
    return jnp.sum((block * block).reshape(block.shape[0] // 8, 8, TILE), axis=0)


def place_left(place_ref, parts, tiles, high_ref, low_ref, lh, ll):
    for r in range(tiles // 2):
        source_rows = pl.ds(pl.multiple_of(place_ref[1 + r] * TILE, TILE), TILE)
        for c in range(parts[0], parts[1]):
            source_cols = pl.ds(pl.multiple_of(place_ref[1 + c] * TILE, TILE), TILE)
            lh[span(r), span(c - parts[0])] = high_ref[source_rows, source_cols]
            ll[span(r), span(c - parts[0])] = low_ref[source_rows, source_cols]


def early_kernel(place_ref, near, xh, xl, out, nh, nl, sum_ref, lh, ll):
    half, size = near.shape
    tiles = size // TILE
    side = place_ref[0]
    total = jnp.zeros((8, TILE), jnp.float32)
    for j in range(tiles):
        block = near[:, span(j)]
        nh[:, span(j)], nl[:, span(j)] = split(block)
        total += squares(block)
    sum_ref[...] = jnp.full(sum_ref.shape, jnp.sum(total), jnp.float32)

    @pl.when(side == 0)
    def _():
        place_left(place_ref, (0, tiles // 2), tiles, xh, xl, lh, ll)
        for j in range(tiles):
            out[:, span(j)] = dot3(lh[...], ll[...], nh[:, span(j)], nl[:, span(j)])

    @pl.when(side != 0)
    def _():
        for j in range(tiles):
            out[:, span(j)] = dot3(nh[...], nl[...], xh[:, span(j)], xl[:, span(j)])


def early_part(place, near, x_high, x_low):
    half, size = near.shape
    square = pltpu.VMEM((half, half), jnp.bfloat16)
    rows = pltpu.HBM((half, size), jnp.bfloat16)
    return pl.pallas_call(
        early_kernel,
        out_shape=[
            pltpu.HBM((half, size), jnp.float32), rows, rows,
            pltpu.HBM((8, 128), jnp.float32),
        ],
        in_specs=[smem()] + [vmem()] * 3,
        out_specs=[vmem()] * 4,
        scratch_shapes=[square, square],
        compiler_params=pltpu.CompilerParams(vmem_limit_bytes=56 * MIB),
        cost_estimate=pl.CostEstimate(flops=0, bytes_accessed=0, transcendentals=0),
        name="early_part",
    )(place, in_hbm(near), in_hbm(x_high), in_hbm(x_low))


def middle_kernel(
    place_ref, near_sum_hbm, far, early_hbm, pack_hbm, yh, yl, sum_ref,
    near_sum, early, pack, xh, xl, fh, fl, lh, ll, sems,
):
    half, size = far.shape
    tiles = size // TILE
    side = place_ref[0]
    pack_load = pltpu.make_async_copy(pack_hbm, pack, sems.at[0])
    early_load = pltpu.make_async_copy(early_hbm, early, sems.at[1])
    sum_load = pltpu.make_async_copy(near_sum_hbm, near_sum, sems.at[2])
    for load in (pack_load, early_load, sum_load):
        load.start()
    total = jnp.zeros((8, TILE), jnp.float32)
    for j in range(tiles):
        block = far[:, span(j)]
        fh[:, span(j)], fl[:, span(j)] = split(block)
        total += squares(block)
    for load in (pack_load, early_load, sum_load):
        load.wait()
    sum_ref[...] = near_sum[...] + jnp.sum(total)

    @pl.when(side == 0)
    def _():
        unpack_left(place_ref, pack, tiles, (tiles // 2, tiles), lh, ll)
        for j in range(tiles):
            column = early[:, span(j)] + dot3(lh[...], ll[...], fh[:, span(j)], fl[:, span(j)])
            yh[:half, span(j)], yl[:half, span(j)] = split(column)

    @pl.when(side != 0)
    def _():
        for j in range(tiles):
            unpack_column(pack, tiles, j, xh, xl)
            yh[:half, span(j)], yl[:half, span(j)] = split(early[:, span(j)])
            column = dot3(fh[...], fl[...], xh[:, span(j)], xl[:, span(j)])
            yh[half:, span(j)], yl[half:, span(j)] = split(column)


def middle_part(place, near_sum, far, early, pack):
    half, size = far.shape
    wide = pltpu.VMEM((half, size), jnp.bfloat16)
    square = pltpu.VMEM((half, half), jnp.bfloat16)
    big = pltpu.VMEM((size, size), jnp.bfloat16)
    return pl.pallas_call(
        middle_kernel,
        out_shape=[big, big, jax.ShapeDtypeStruct((8, 128), jnp.float32)],
        in_specs=[smem(), anywhere(), vmem(), anywhere(), anywhere()],
        out_specs=[vmem()] * 3,
        scratch_shapes=[
            pltpu.VMEM(near_sum.shape, jnp.float32),
            pltpu.VMEM((half, size), jnp.float32),
            pltpu.VMEM(pack.shape, jnp.float32),
            big, big, wide, wide, square, square,
            pltpu.SemaphoreType.DMA((3,)),
        ],
        compiler_params=pltpu.CompilerParams(vmem_limit_bytes=24 * MIB),
        cost_estimate=pl.CostEstimate(flops=0, bytes_accessed=0, transcendentals=0),
        name="middle_part",
    )(place, in_hbm(near_sum), resident(far), in_hbm(early), in_hbm(pack))


def last_kernel(place_ref, grad_sum_ref, yh, yl, pack, raw, sums_ref, ph, pw, lh, ll):
    half, size = raw.shape
    tiles = size // TILE
    side = place_ref[0]

    def multiply(ah, al, bh, bl, prepare):
        total = jnp.zeros((8, TILE), jnp.float32)
        for j in range(tiles):
            prepare(j)
            column = dot3(ah, al, bh[:, span(j)], bl[:, span(j)])
            raw[:, span(j)] = column
            total += squares(column)
        lane = lax.broadcasted_iota(jnp.int32, (8, 128), 1)
        sums_ref[...] = jnp.where(lane == 0, jnp.sum(total), grad_sum_ref[...])

    @pl.when(side == 0)
    def _():
        multiply(yh[:half], yl[:half], ph, pw, lambda j: unpack_column(pack, tiles, j, ph, pw))

    @pl.when(side != 0)
    def _():
        unpack_left(place_ref, pack, tiles, (0, tiles), lh, ll)
        multiply(lh[...], ll[...], yh, yl, lambda j: None)


def last_part(place, grad_sum, y_high, y_low, pack):
    size = y_high.shape[0]
    half = size // 2
    wide = pltpu.VMEM((half, size), jnp.bfloat16)
    big = pltpu.VMEM((size, size), jnp.bfloat16)
    return pl.pallas_call(
        last_kernel,
        out_shape=[
            pltpu.VMEM((half, size), jnp.float32),
            jax.ShapeDtypeStruct((8, 128), jnp.float32),
        ],
        in_specs=[smem()] + [vmem()] * 4,
        out_specs=[vmem(), vmem()],
        scratch_shapes=[big, big, wide, wide],
        compiler_params=pltpu.CompilerParams(vmem_limit_bytes=32 * MIB),
        cost_estimate=pl.CostEstimate(
            flops=3 * size**3, bytes_accessed=12 * 2**20, transcendentals=0
        ),
        name="last_part",
    )(place, grad_sum, resident(y_high), resident(y_low), resident(pack))


def graft_kernel(own_ref, other_ref, raw, out_hbm, buffer, sems):
    half, size = buffer.shape
    steps = sems.shape[0]
    count = size * size
    own = own_ref[...]
    raw_sum = own[:1, :1] + other_ref[:1, :1]
    grad_sum = own[:1, 1:2]
    scale = jnp.sqrt(grad_sum / count + epsilon) / jnp.sqrt(raw_sum / count + epsilon)
    stores = []
    for k in range(steps):
        rows = slice(k * half // steps, (k + 1) * half // steps)
        buffer[rows] = raw[rows] * scale
        stores.append(pltpu.make_async_copy(buffer.at[rows], out_hbm.at[rows], sems.at[k]))
        stores[-1].start()
    for store in stores:
        store.wait()


def graft(own_sums, other_sums, raw):
    steps = 4
    return pl.pallas_call(
        graft_kernel,
        out_shape=pltpu.HBM(raw.shape, jnp.float32),
        in_specs=[vmem(), vmem(), vmem()],
        out_specs=anywhere(),
        scratch_shapes=[
            pltpu.VMEM(raw.shape, jnp.float32),
            pltpu.SemaphoreType.DMA((steps,)),
        ],
        compiler_params=pltpu.CompilerParams(vmem_limit_bytes=6 * MIB),
        cost_estimate=pl.CostEstimate(flops=0, bytes_accessed=4 * 2**20, transcendentals=0),
        name="graft",
    )(own_sums, other_sums, resident(raw))


def renew_kernel(place_ref, a_ref, nh_ref, nl_ref, far_ref, out_ref, high_ref, low_ref):
    size = a_ref.shape[0]
    half = size // 2
    tiles = size // TILE
    side = place_ref[0]
    used = place_ref[1 + tiles] != 0

    for p in range(tiles):
        for c in range(tiles):
            if p < half // TILE:
                high, low = nh_ref[span(p), span(c)], nl_ref[span(p), span(c)]
            else:
                high, low = split(far_ref[span(p - half // TILE), span(c)])
            for block, target in ((high, high_ref), (low, low_ref)):
                target[side, span(p), span(c)] = block
                target[1 - side, span(c), span(p)] = block.T

    def write(i, j, block):
        i, j = (jnp.where(side == 0, place_ref[1 + k], k) for k in (i, j))
        rows = pl.ds(pl.multiple_of(i * TILE, TILE), TILE)
        cols = pl.ds(pl.multiple_of(j * TILE, TILE), TILE)
        gain = jnp.where(used, block * ((1.0 - decay_rate) / size), 0.0)
        out_ref[rows, cols] = decay_rate * a_ref[rows, cols] + gain

    for j in range(tiles):
        low_rows = slice(j * TILE, size)
        column = dot3(
            high_ref[0, low_rows, :], low_ref[0, low_rows, :],
            high_ref[1, :, span(j)], low_ref[1, :, span(j)],
        )
        for i in range(j, tiles):
            block = column[span(i - j)]
            write(i, j, block)
            if i != j:
                write(j, i, block.T)


def renew(place, factor, near_high, near_low, far):
    size = factor.shape[0]
    return pl.pallas_call(
        renew_kernel,
        out_shape=jax.ShapeDtypeStruct((size, size), jnp.float32),
        in_specs=[smem()] + [vmem()] * 4,
        out_specs=vmem(),
        scratch_shapes=[pltpu.VMEM((2, size, size), jnp.bfloat16)] * 2,
        compiler_params=pltpu.CompilerParams(vmem_limit_bytes=56 * MIB),
        cost_estimate=pl.CostEstimate(
            flops=4 * size**3, bytes_accessed=12 * 2**20, transcendentals=0
        ),
        name="renew",
    )(place, factor, near_high, near_low, far)


def per_device(grad, factors, owners):
    row_count = grad.shape[0]
    block_size = factors.shape[-1]
    owner_count = lax.axis_size("block")
    dp_index = lax.axis_index("dp")
    blk_index = lax.axis_index("block")
    side = dp_index % 2
    slot = dp_index // 2
    outer_pair = (dp_index == 0) | (dp_index == 3)
    groups = [
        [x * owner_count + b for x in pair for b in range(owner_count)] for pair in ((0, 3), (1, 2))
    ]

    def exchange(x):
        return lax.all_to_all(
            x, BOTH, split_axis=0, concat_axis=0, tiled=True, axis_index_groups=groups
        )

    def swap(x):
        return lax.ppermute(x, "dp", [(i, i ^ 1) for i in range(4)])

    order = jnp.where(outer_pair, jnp.array(OUTER_ORDER), jnp.array(INNER_ORDER))
    used = jnp.sum(owners == blk_index) > slot
    place = jnp.concatenate([side[None], order, used[None]]).astype(jnp.int32)

    near = exchange(deal(owners, grad, owner_count, False)).reshape(block_size // 2, block_size)
    other_grad = swap(grad)
    own_factor = factors[0, 0]
    x_high, x_low, pack = root(own_factor)
    pack, other_grad = lax.optimization_barrier((pack, other_grad))
    other_pack = swap(pack)
    dealt = deal(owners, other_grad, owner_count, True)
    near, dealt = lax.optimization_barrier((near, dealt))
    far = exchange(dealt).reshape(block_size // 2, block_size)

    early, near_high, near_low, near_sum = early_part(place, near, x_high, x_low)
    y_high, y_low, grad_sum = middle_part(place, near_sum, far, early, pack)
    raw, sums = last_part(place, grad_sum, y_high, y_low, other_pack)
    scaled = graft(sums, swap(sums), raw)
    scaled, far = lax.optimization_barrier((scaled, far))
    back = exchange(scaled.reshape(2 * owner_count, row_count, block_size))
    update = collect(owners, back)
    new_own = renew(place, own_factor, near_high, near_low, far)
    return (new_own[None, None], update)


def solution(mesh):
    placed = (P(BOTH, None), P("dp", "block", None, None), P())
    return jax.shard_map(
        per_device,
        mesh=mesh,
        in_specs=placed,
        out_specs=(P("dp", "block", None, None), P(BOTH, None)),
        check_vma=False,
    )
```

profile of v0, /device:TPU:1, one launch (start us, length us, event | category | flops | bytes accessed | tf_op | source)
XLA Modules:
  0.0 137.6 jit_solution(3726209495484615593)
XLA Ops:
  0.6 2.1 %collective-permute-start = (f32[8,28672]{1,0:T(8,128)}, f32[8,28672]{1,0:T(8,128)S(1)}, u32[]{:S(2)}, u32[]{:S(2)}) collective-permute-start(f32[8,28672]{1,0:T(8,128)} %grad_hbm.1), channel_id=1, source_target_pairs={{0,32},{32,0},{64,96},{96,64},{1,33},{33,1},{65,97},{97,65},{2,34}... | collective-permute-start | bytes 2752520 | tf_op jit(solution)/shard_map/ppermute | solution.py:569
  2.7 0.0 copy-start.2
  2.8 0.7 copy-done.2
  3.4 2.7 %deal.2 = f32[64,8,1024]{2,1,0:T(8,128)} custom-call(s32[28]{0:T(128)S(1)} %copy-done.2, f32[8,28672]{1,0:T(8,128)} %grad_hbm.1), custom_call_target="tpu_custom_call" | custom-call | flops 49999998976 | bytes 4194304 | tf_op jit(solution)/shard_map/deal/pallas_call | solution.py:124
  6.1 11.2 %all-to-all-start = ((f32[64,8,1024]{2,1,0:T(8,128)}), f32[64,8,1024]{2,1,0:T(8,128)}, u32[]{:S(2)}, u32[]{:S(2)}) async-start(f32[64,8,1024]{2,1,0:T(8,128)} %deal.2), calls=%async_computation | async-start | bytes 4194304 | tf_op jit(solution)/shard_map/all_to_all | solution.py:564
  17.3 0.0 copy-start.3
  17.3 17.0 %root.1 = (bf16[1024,1024]{1,0:T(8,128)(2,1)}, bf16[1024,1024]{1,0:T(8,128)(2,1)}, f32[2064,256]{1,0:T(8,128)}) custom-call(f32[1024,1024]{1,0:T(8,128)} %bitcast.10), custom_call_target="tpu_custom_call" | custom-call | tf_op jit(solution)/shard_map/root/pallas_call | solution.py:250
  34.3 0.0 collective-permute-done.grad
  34.3 0.4 collective-permute-start.1
  34.7 0.0 copy-done.3
  34.7 1.7 %deal.3 = f32[64,8,1024]{2,1,0:T(8,128)} custom-call(s32[28]{0:T(128)S(1)} %copy-done.3, f32[8,28672]{1,0:T(8,128)S(1)} %collective-permute-done.grad), custom_call_target="tpu_custom_call" | custom-call | flops 49999998976 | bytes 4194304 | tf_op jit(solution)/shard_map/deal/pallas_call | solution.py:124
  36.4 9.6 %all-to-all-done = f32[64,8,1024]{2,1,0:T(8,128)} async-done(((f32[64,8,1024]{2,1,0:T(8,128)}), f32[64,8,1024]{2,1,0:T(8,128)}, u32[]{:S(2)}, u32[]{:S(2)}) %all-to-all-start) | async-done | bytes 2097184 | tf_op jit(solution)/shard_map/all_to_all | solution.py:564
  46.0 0.0 copy-start.4
  46.0 0.0 copy-start.5
  46.0 7.0 %all-to-all-start.1 = ((f32[64,8,1024]{2,1,0:T(8,128)}), f32[64,8,1024]{2,1,0:T(8,128)S(1)}, u32[]{:S(2)}, u32[]{:S(2)}) async-start(f32[64,8,1024]{2,1,0:T(8,128)} %deal.3), calls=%async_computation.1 | async-start | bytes 4194304 | tf_op jit(solution)/shard_map/all_to_all | solution.py:564
  53.0 0.6 fusion
  54.3 0.0 copy-done.4
  54.3 0.0 copy-done.5
  54.3 0.6 pad_add_fusion.place_ref
  54.9 0.0 copy-start.1
  54.9 7.7 %early_part.1 = (f32[512,1024]{1,0:T(8,128)}, bf16[512,1024]{1,0:T(8,128)(2,1)}, bf16[512,1024]{1,0:T(8,128)(2,1)}, f32[8,128]{1,0:T(8,128)}) custom-call(s32[6]{0:T(128)} %pad_add_fusion.place_ref, f32[512,1024]{1,0:T(8,128)} %bitcast.3.near, bf16[1024,1024]{1,0:T(8,128)(2,1)} %get-tuple-element.23.xh, bf16[1024,1024]{1,0:T(8,128)(2,1)} %get-tuple-element.24.xl), custom_call_target="tpu_custom_call" | custom-call | tf_op jit(solution)/shard_map/early_part/pallas_call | solution.py:340
  62.6 19.1 %all-to-all-done.1 = f32[64,8,1024]{2,1,0:T(8,128)S(1)} async-done(((f32[64,8,1024]{2,1,0:T(8,128)}), f32[64,8,1024]{2,1,0:T(8,128)S(1)}, u32[]{:S(2)}, u32[]{:S(2)}) %all-to-all-start.1) | async-done | bytes 2097184 | tf_op jit(solution)/shard_map/all_to_all | solution.py:564
  81.7 0.0 copy-start
  81.7 0.0 copy-done.1
  81.7 5.2 %middle_part.1 = (bf16[1024,1024]{1,0:T(8,128)(2,1)S(1)}, bf16[1024,1024]{1,0:T(8,128)(2,1)S(1)}, f32[8,128]{1,0:T(8,128)S(1)}) custom-call(s32[6]{0:T(128)S(1)} %copy-done.1, f32[8,128]{1,0:T(8,128)} %get-tuple-element.27.near_sum_hbm, f32[512,1024]{1,0:T(8,128)S(1)} %bitcast.7, f32[512,1024]{1,0:T(8,128)} %get-tuple-element.29.early_hbm, ...), custom_call_target="tpu_custom_call" | custom-call | tf_op jit(solution)/shard_map/middle_part/pallas_call | solution.py:397
  86.9 0.0 copy-done
  86.9 0.0 collective-permute-done.1.pack
  86.9 5.6 %last_part.1 = (f32[512,1024]{1,0:T(8,128)S(1)}, f32[8,128]{1,0:T(8,128)S(1)}) custom-call(s32[6]{0:T(128)S(1)} %copy-done.1, f32[8,128]{1,0:T(8,128)S(1)} %get-tuple-element.31.grad_sum_ref, bf16[1024,1024]{1,0:T(8,128)(2,1)S(1)} %get-tuple-element.32.yh, bf16[1024,1024]{1,0:T(8,128)(2,1)S(1)} %get-tuple-element.33.yl, f32[2064,256]{1,0:T(8,128)} %collective-permute-done.1.pack), custom_call_target="tpu_custom_call" | custom-call | flops 3221225472 | bytes 12582912 | tf_op jit(solution)/shard_map/last_part/pallas_call | solution.py:445
  92.5 1.4 %collective-permute-start.2 = (f32[8,128]{1,0:T(8,128)S(1)}, f32[8,128]{1,0:T(8,128)S(1)}, u32[]{:S(2)}, u32[]{:S(2)}) collective-permute-start(f32[8,128]{1,0:T(8,128)S(1)} %get-tuple-element.34.own_ref), channel_id=1, source_target_pairs={{0,32},{32,0},{64,96},{96,64},{1,33},{33,1},{65,97},{97,65},{2,34}... | collective-permute-start | bytes 12296 | tf_op jit(solution)/shard_map/ppermute | solution.py:569
  93.9 1.1 collective-permute-done.2.other_ref
  95.1 1.6 %graft.1 = f32[512,1024]{1,0:T(8,128)} custom-call(f32[8,128]{1,0:T(8,128)S(1)} %get-tuple-element.34.own_ref, f32[8,128]{1,0:T(8,128)S(1)} %collective-permute-done.2.other_ref, f32[512,1024]{1,0:T(8,128)S(1)} %get-tuple-element.35.raw), custom_call_target="tpu_custom_call" | custom-call | bytes 4194304 | tf_op jit(solution)/shard_map/graft/pallas_call | solution.py:482
  96.7 10.3 %all-to-all-start.2 = ((f32[64,8,1024]{2,1,0:T(8,128)}), f32[64,8,1024]{2,1,0:T(8,128)S(1)}, u32[]{:S(2)}, u32[]{:S(2)}) async-start(f32[64,8,1024]{2,1,0:T(8,128)} %bitcast.9), calls=%async_computation.2 | async-start | bytes 4194304 | tf_op jit(solution)/shard_map/all_to_all | solution.py:564
  107.0 11.8 %renew.1 = f32[1024,1024]{1,0:T(8,128)} custom-call(s32[6]{0:T(128)} %pad_add_fusion.place_ref, f32[1024,1024]{1,0:T(8,128)} %bitcast.11, bf16[512,1024]{1,0:T(8,128)(2,1)} %get-tuple-element.25.nh_ref, bf16[512,1024]{1,0:T(8,128)(2,1)} %get-tuple-element.26.nl_ref, f32[512,1024]{1,0:T(8,128)} %bitcast.8), custom_call_target="tpu_custom_call" | custom-call | flops 4294967296 | bytes 12582912 | tf_op jit(solution)/shard_map/renew/pallas_call | solution.py:536
  118.8 16.9 %all-to-all-done.2.back = f32[64,8,1024]{2,1,0:T(8,128)S(1)} async-done(((f32[64,8,1024]{2,1,0:T(8,128)}), f32[64,8,1024]{2,1,0:T(8,128)S(1)}, u32[]{:S(2)}, u32[]{:S(2)}) %all-to-all-start.2) | async-done | bytes 2097184 | tf_op jit(solution)/shard_map/all_to_all | solution.py:564
  135.8 1.7 %collect.1 = f32[8,28672]{1,0:T(8,128)} custom-call(s32[28]{0:T(128)S(1)} %copy-done.3, f32[64,8,1024]{2,1,0:T(8,128)S(1)} %all-to-all-done.2.back), custom_call_target="tpu_custom_call" | custom-call | bytes 4194304 | tf_op jit(solution)/shard_map/collect/pallas_call | solution.py:138
  (1 shorter events, 0.0 us)
Async XLA Ops:
  0.6 33.6 %collective-permute-start = (f32[8,28672]{1,0:T(8,128)}, f32[8,28672]{1,0:T(8,128)S(1)}, u32[]{:S(2)}, u32[]{:S(2)}) collective-permute-start(f32[8,28672]{1,0:T(8,128)} %grad_hbm.1), channel_id=1, source_target_pairs={{0,32},{32,0},{64,96},{96,64},{1,33},{33,1},{65,97},{97,65},{2,34}... | collective-permute-start | bytes 2752520 | tf_op jit(solution)/shard_map/ppermute | solution.py:569
  2.7 0.7 copy-start.2
  6.1 39.9 %all-to-all-start = ((f32[64,8,1024]{2,1,0:T(8,128)}), f32[64,8,1024]{2,1,0:T(8,128)}, u32[]{:S(2)}, u32[]{:S(2)}) async-start(f32[64,8,1024]{2,1,0:T(8,128)} %deal.2), calls=%async_computation | async-start | bytes 4194304 | tf_op jit(solution)/shard_map/all_to_all | solution.py:564
  17.3 17.4 %copy-start.3 = (s32[28]{0:T(128)S(1)}, s32[28]{0:T(128)}, u32[]{:S(2)}) copy-start(s32[28]{0:T(128)} %owners_ref.5) | copy-start | bytes 340
  34.3 52.7 %collective-permute-start.1 = (f32[2064,256]{1,0:T(8,128)}, f32[2064,256]{1,0:T(8,128)}, u32[]{:S(2)}, u32[]{:S(2)}) collective-permute-start(f32[2064,256]{1,0:T(8,128)} %get-tuple-element.30.pack_hbm), channel_id=1, source_target_pairs={{0,32},{32,0},{64,96},{96,64},{1,33},{33,1},{65,97},{97,65},{2,34}... | collective-permute-start | bytes 6340616 | tf_op jit(solution)/shard_map/ppermute | solution.py:569
  46.0 8.3 %copy-start.4 = (s32[4]{0:T(128)S(1)}, s32[4]{0:T(128)}, u32[]{:S(2)}) copy-start(s32[4]{0:T(128)} %constant.41.clone) | copy-start | bytes 52
  46.0 8.3 %copy-start.5 = (s32[4]{0:T(128)S(1)}, s32[4]{0:T(128)}, u32[]{:S(2)}) copy-start(s32[4]{0:T(128)} %constant.40.clone) | copy-start | bytes 52
  46.0 35.7 %all-to-all-start.1 = ((f32[64,8,1024]{2,1,0:T(8,128)}), f32[64,8,1024]{2,1,0:T(8,128)S(1)}, u32[]{:S(2)}, u32[]{:S(2)}) async-start(f32[64,8,1024]{2,1,0:T(8,128)} %deal.3), calls=%async_computation.1 | async-start | bytes 4194304 | tf_op jit(solution)/shard_map/all_to_all | solution.py:564
  54.9 26.8 %copy-start.1 = (s32[6]{0:T(128)S(1)}, s32[6]{0:T(128)}, u32[]{:S(2)}) copy-start(s32[6]{0:T(128)} %pad_add_fusion.place_ref) | copy-start | bytes 76
  81.7 5.2 %copy-start = (f32[64,8,1024]{2,1,0:T(8,128)}, f32[64,8,1024]{2,1,0:T(8,128)S(1)}, u32[]{:S(2)}) copy-start(f32[64,8,1024]{2,1,0:T(8,128)S(1)} %all-to-all-done.1) | copy-start | bytes 6291460
  92.5 2.5 %collective-permute-start.2 = (f32[8,128]{1,0:T(8,128)S(1)}, f32[8,128]{1,0:T(8,128)S(1)}, u32[]{:S(2)}, u32[]{:S(2)}) collective-permute-start(f32[8,128]{1,0:T(8,128)S(1)} %get-tuple-element.34.own_ref), channel_id=1, source_target_pairs={{0,32},{32,0},{64,96},{96,64},{1,33},{33,1},{65,97},{97,65},{2,34}... | collective-permute-start | bytes 12296 | tf_op jit(solution)/shard_map/ppermute | solution.py:569
  96.7 39.1 %all-to-all-start.2 = ((f32[64,8,1024]{2,1,0:T(8,128)}), f32[64,8,1024]{2,1,0:T(8,128)S(1)}, u32[]{:S(2)}, u32[]{:S(2)}) async-start(f32[64,8,1024]{2,1,0:T(8,128)} %bitcast.9), calls=%async_computation.2 | async-start | bytes 4194304 | tf_op jit(solution)/shard_map/all_to_all | solution.py:564
where the time goes:
time: 138 us
  Pallas kernels  54.9 us (40%)
  waiting for transfers between devices  46.8 us (34%)
  starting transfers between devices  32.4 us (23%)
  between operations  1.63 us (1%)
    all_to_all x3, waiting for transfers between devices, exchange(): lax.all_to_all(x, BOTH, split_axis=0, concat_axis=0, tiled=True, axis_ind...  45.6 us
    all_to_all x3, starting transfers between devices, exchange(): lax.all_to_all(x, BOTH, split_axis=0, concat_axis=0, tiled=True, axis_ind...  28.5 us
    pallas_call x1, Pallas kernels, root(): pl.pallas_call(root_kernel, out_shape=[half, half, pltpu.HBM(packed, jnp....  17 us
    pallas_call x1, Pallas kernels, renew(): pl.pallas_call(renew_kernel, out_shape=jax.ShapeDtypeStruct((size, size),...  11.8 us
    pallas_call x1, Pallas kernels, early_part(): pl.pallas_call(early_kernel, out_shape=[pltpu.HBM((half, size), jnp.float...  7.68 us
    pallas_call x1, Pallas kernels, last_part(): pl.pallas_call(last_kernel, out_shape=[pltpu.VMEM((half, size), jnp.float...  5.57 us
    pallas_call x1, Pallas kernels, middle_part(): pl.pallas_call(middle_kernel, out_shape=[big, big, jax.ShapeDtypeStruct((...  5.2 us
    pallas_call x2, Pallas kernels, deal(): pl.pallas_call(deal_resident_kernel if landed else deal_kernel, out_shape...  4.35 us
  transfers between devices with their start and end apart: 6, of which 4 were waited for; matrix products, arithmetic and copies ran while one was open for 1% of the time, Pallas kernels for 33%

commit v1 on v0

--- a/solution.py
+++ b/solution.py
@@ -130,7 +130,7 @@
         compiler_params=pltpu.CompilerParams(vmem_limit_bytes=16 * MIB),
         cost_estimate=pl.CostEstimate(flops=5 * 10**10, bytes_accessed=2**22, transcendentals=0),
         name="deal",
-    )(owners, resident(grad) if landed else in_hbm(grad))
+    )(owners if landed else in_hbm(owners), resident(grad) if landed else in_hbm(grad))
 
 
 def collect(owners, back):
@@ -369,13 +369,14 @@
         block = far[:, span(j)]
         fh[:, span(j)], fl[:, span(j)] = split(block)
         total += squares(block)
-    for load in (pack_load, early_load, sum_load):
+    for load in (pack_load, sum_load):
         load.wait()
     sum_ref[...] = near_sum[...] + jnp.sum(total)
 
     @pl.when(side == 0)
     def _():
         unpack_left(place_ref, pack, tiles, (tiles // 2, tiles), lh, ll)
+        early_load.wait()
         for j in range(tiles):
             column = early[:, span(j)] + dot3(lh[...], ll[...], fh[:, span(j)], fl[:, span(j)])
             yh[:half, span(j)], yl[:half, span(j)] = split(column)
@@ -384,9 +385,11 @@
     def _():
         for j in range(tiles):
             unpack_column(pack, tiles, j, xh, xl)
-            yh[:half, span(j)], yl[:half, span(j)] = split(early[:, span(j)])
             column = dot3(fh[...], fl[...], xh[:, span(j)], xl[:, span(j)])
             yh[half:, span(j)], yl[half:, span(j)] = split(column)
+        early_load.wait()
+        for j in range(tiles):
+            yh[:half, span(j)], yl[:half, span(j)] = split(early[:, span(j)])
 
 
 def middle_part(place, near_sum, far, early, pack):

time: 138 us -> 137 us (level)
  transfers between devices with their start and end apart: 6 -> 6, of which waited for: 4 -> 4; matrix products, arithmetic and copies ran while one was open for 1% -> 1% of each run, Pallas kernels for 33% -> 34%
where the time goes in v1:
time: 137 us
  Pallas kernels  54.8 us (40%)
  waiting for transfers between devices  46.8 us (34%)
  starting transfers between devices  32.2 us (24%)
  between operations  1.63 us (1%)
    all_to_all x3, waiting for transfers between devices, exchange(): lax.all_to_all(x, BOTH, split_axis=0, concat_axis=0, tiled=True, axis_ind...  45.6 us
    all_to_all x3, starting transfers between devices, exchange(): lax.all_to_all(x, BOTH, split_axis=0, concat_axis=0, tiled=True, axis_ind...  28.4 us
    pallas_call x1, Pallas kernels, root(): pl.pallas_call(root_kernel, out_shape=[half, half, pltpu.HBM(packed, jnp....  17 us
    pallas_call x1, Pallas kernels, renew(): pl.pallas_call(renew_kernel, out_shape=jax.ShapeDtypeStruct((size, size),...  11.8 us
    pallas_call x1, Pallas kernels, early_part(): pl.pallas_call(early_kernel, out_shape=[pltpu.HBM((half, size), jnp.float...  7.65 us
    pallas_call x1, Pallas kernels, last_part(): pl.pallas_call(last_kernel, out_shape=[pltpu.VMEM((half, size), jnp.float...  5.57 us
    pallas_call x1, Pallas kernels, middle_part(): pl.pallas_call(middle_kernel, out_shape=[big, big, jax.ShapeDtypeStruct((...  4.92 us
    pallas_call x2, Pallas kernels, deal(): pl.pallas_call(deal_resident_kernel if landed else deal_kernel, out_shape...  4.56 us
  transfers between devices with their start and end apart: 6, of which 4 were waited for; matrix products, arithmetic and copies ran while one was open for 1% of the time, Pallas kernels for 34%

profile of v1, /device:TPU:1, one launch (start us, length us, event | category | flops | bytes accessed | tf_op | source)
XLA Modules:
  0.0 136.7 jit_solution(7891942647802648983)
XLA Ops:
  0.6 2.1 %collective-permute-start = (f32[8,28672]{1,0:T(8,128)}, f32[8,28672]{1,0:T(8,128)S(1)}, u32[]{:S(2)}, u32[]{:S(2)}) collective-permute-start(f32[8,28672]{1,0:T(8,128)} %grad_hbm.1), channel_id=1, source_target_pairs={{0,32},{32,0},{64,96},{96,64},{1,33},{33,1},{65,97},{97,65},{2,34}... | collective-permute-start | bytes 2752520 | tf_op jit(solution)/shard_map/ppermute | solution.py:572
  2.7 2.8 %deal.2 = f32[64,8,1024]{2,1,0:T(8,128)} custom-call(s32[28]{0:T(128)} %owners_ref.5, f32[8,28672]{1,0:T(8,128)} %grad_hbm.1), custom_call_target="tpu_custom_call" | custom-call | flops 49999998976 | bytes 4194304 | tf_op jit(solution)/shard_map/deal/pallas_call | solution.py:124
  5.6 11.2 %all-to-all-start = ((f32[64,8,1024]{2,1,0:T(8,128)}), f32[64,8,1024]{2,1,0:T(8,128)}, u32[]{:S(2)}, u32[]{:S(2)}) async-start(f32[64,8,1024]{2,1,0:T(8,128)} %deal.2), calls=%async_computation | async-start | bytes 4194304 | tf_op jit(solution)/shard_map/all_to_all | solution.py:567
  16.8 0.0 copy-start.2
  16.8 17.0 %root.1 = (bf16[1024,1024]{1,0:T(8,128)(2,1)}, bf16[1024,1024]{1,0:T(8,128)(2,1)}, f32[2064,256]{1,0:T(8,128)}) custom-call(f32[1024,1024]{1,0:T(8,128)} %bitcast.10), custom_call_target="tpu_custom_call" | custom-call | tf_op jit(solution)/shard_map/root/pallas_call | solution.py:250
  33.7 0.0 collective-permute-done.grad
  33.8 0.4 collective-permute-start.1
  34.2 0.0 copy-done.2
  34.2 1.8 %deal.3 = f32[64,8,1024]{2,1,0:T(8,128)} custom-call(s32[28]{0:T(128)S(1)} %copy-done.2, f32[8,28672]{1,0:T(8,128)S(1)} %collective-permute-done.grad), custom_call_target="tpu_custom_call" | custom-call | flops 49999998976 | bytes 4194304 | tf_op jit(solution)/shard_map/deal/pallas_call | solution.py:124
  35.9 9.5 %all-to-all-done = f32[64,8,1024]{2,1,0:T(8,128)} async-done(((f32[64,8,1024]{2,1,0:T(8,128)}), f32[64,8,1024]{2,1,0:T(8,128)}, u32[]{:S(2)}, u32[]{:S(2)}) %all-to-all-start) | async-done | bytes 2097184 | tf_op jit(solution)/shard_map/all_to_all | solution.py:567
  45.4 0.0 copy-start.3
  45.4 0.0 copy-start.4
  45.4 7.0 %all-to-all-start.1 = ((f32[64,8,1024]{2,1,0:T(8,128)}), f32[64,8,1024]{2,1,0:T(8,128)S(1)}, u32[]{:S(2)}, u32[]{:S(2)}) async-start(f32[64,8,1024]{2,1,0:T(8,128)} %deal.3), calls=%async_computation.1 | async-start | bytes 4194304 | tf_op jit(solution)/shard_map/all_to_all | solution.py:567
  52.4 0.6 fusion
  53.7 0.0 copy-done.3
  53.8 0.0 copy-done.4
  53.8 0.6 pad_add_fusion.place_ref
  54.4 0.0 copy-start.1
  54.4 7.6 %early_part.1 = (f32[512,1024]{1,0:T(8,128)}, bf16[512,1024]{1,0:T(8,128)(2,1)}, bf16[512,1024]{1,0:T(8,128)(2,1)}, f32[8,128]{1,0:T(8,128)}) custom-call(s32[6]{0:T(128)} %pad_add_fusion.place_ref, f32[512,1024]{1,0:T(8,128)} %bitcast.3.near, bf16[1024,1024]{1,0:T(8,128)(2,1)} %get-tuple-element.23.xh, bf16[1024,1024]{1,0:T(8,128)(2,1)} %get-tuple-element.24.xl), custom_call_target="tpu_custom_call" | custom-call | tf_op jit(solution)/shard_map/early_part/pallas_call | solution.py:340
  62.0 19.2 %all-to-all-done.1 = f32[64,8,1024]{2,1,0:T(8,128)S(1)} async-done(((f32[64,8,1024]{2,1,0:T(8,128)}), f32[64,8,1024]{2,1,0:T(8,128)S(1)}, u32[]{:S(2)}, u32[]{:S(2)}) %all-to-all-start.1) | async-done | bytes 2097184 | tf_op jit(solution)/shard_map/all_to_all | solution.py:567
  81.2 0.0 copy-start
  81.2 0.0 copy-done.1
  81.2 4.9 %middle_part.1 = (bf16[1024,1024]{1,0:T(8,128)(2,1)S(1)}, bf16[1024,1024]{1,0:T(8,128)(2,1)S(1)}, f32[8,128]{1,0:T(8,128)S(1)}) custom-call(s32[6]{0:T(128)S(1)} %copy-done.1, f32[8,128]{1,0:T(8,128)} %get-tuple-element.27.near_sum_hbm, f32[512,1024]{1,0:T(8,128)S(1)} %bitcast.7, f32[512,1024]{1,0:T(8,128)} %get-tuple-element.29.early_hbm, ...), custom_call_target="tpu_custom_call" | custom-call | tf_op jit(solution)/shard_map/middle_part/pallas_call | solution.py:400
  86.1 0.0 copy-done
  86.1 0.0 collective-permute-done.1.pack
  86.1 5.6 %last_part.1 = (f32[512,1024]{1,0:T(8,128)S(1)}, f32[8,128]{1,0:T(8,128)S(1)}) custom-call(s32[6]{0:T(128)S(1)} %copy-done.1, f32[8,128]{1,0:T(8,128)S(1)} %get-tuple-element.31.grad_sum_ref, bf16[1024,1024]{1,0:T(8,128)(2,1)S(1)} %get-tuple-element.32.yh, bf16[1024,1024]{1,0:T(8,128)(2,1)S(1)} %get-tuple-element.33.yl, f32[2064,256]{1,0:T(8,128)} %collective-permute-done.1.pack), custom_call_target="tpu_custom_call" | custom-call | flops 3221225472 | bytes 12582912 | tf_op jit(solution)/shard_map/last_part/pallas_call | solution.py:448
  91.7 1.3 collective-permute-start.2
  93.0 1.2 collective-permute-done.2.other_ref
  94.3 1.6 %graft.1 = f32[512,1024]{1,0:T(8,128)} custom-call(f32[8,128]{1,0:T(8,128)S(1)} %get-tuple-element.34.own_ref, f32[8,128]{1,0:T(8,128)S(1)} %collective-permute-done.2.other_ref, f32[512,1024]{1,0:T(8,128)S(1)} %get-tuple-element.35.raw), custom_call_target="tpu_custom_call" | custom-call | bytes 4194304 | tf_op jit(solution)/shard_map/graft/pallas_call | solution.py:485
  95.9 10.2 %all-to-all-start.2 = ((f32[64,8,1024]{2,1,0:T(8,128)}), f32[64,8,1024]{2,1,0:T(8,128)S(1)}, u32[]{:S(2)}, u32[]{:S(2)}) async-start(f32[64,8,1024]{2,1,0:T(8,128)} %bitcast.9), calls=%async_computation.2 | async-start | bytes 4194304 | tf_op jit(solution)/shard_map/all_to_all | solution.py:567
  106.1 11.8 %renew.1 = f32[1024,1024]{1,0:T(8,128)} custom-call(s32[6]{0:T(128)} %pad_add_fusion.place_ref, f32[1024,1024]{1,0:T(8,128)} %bitcast.11, bf16[512,1024]{1,0:T(8,128)(2,1)} %get-tuple-element.25.nh_ref, bf16[512,1024]{1,0:T(8,128)(2,1)} %get-tuple-element.26.nl_ref, f32[512,1024]{1,0:T(8,128)} %bitcast.8), custom_call_target="tpu_custom_call" | custom-call | flops 4294967296 | bytes 12582912 | tf_op jit(solution)/shard_map/renew/pallas_call | solution.py:539
  118.0 16.9 %all-to-all-done.2.back = f32[64,8,1024]{2,1,0:T(8,128)S(1)} async-done(((f32[64,8,1024]{2,1,0:T(8,128)}), f32[64,8,1024]{2,1,0:T(8,128)S(1)}, u32[]{:S(2)}, u32[]{:S(2)}) %all-to-all-start.2) | async-done | bytes 2097184 | tf_op jit(solution)/shard_map/all_to_all | solution.py:567
  134.9 1.7 %collect.1 = f32[8,28672]{1,0:T(8,128)} custom-call(s32[28]{0:T(128)S(1)} %copy-done.2, f32[64,8,1024]{2,1,0:T(8,128)S(1)} %all-to-all-done.2.back), custom_call_target="tpu_custom_call" | custom-call | bytes 4194304 | tf_op jit(solution)/shard_map/collect/pallas_call | solution.py:138
  (1 shorter events, 0.0 us)
Async XLA Ops:
  0.6 33.1 %collective-permute-start = (f32[8,28672]{1,0:T(8,128)}, f32[8,28672]{1,0:T(8,128)S(1)}, u32[]{:S(2)}, u32[]{:S(2)}) collective-permute-start(f32[8,28672]{1,0:T(8,128)} %grad_hbm.1), channel_id=1, source_target_pairs={{0,32},{32,0},{64,96},{96,64},{1,33},{33,1},{65,97},{97,65},{2,34}... | collective-permute-start | bytes 2752520 | tf_op jit(solution)/shard_map/ppermute | solution.py:572
  5.6 39.9 %all-to-all-start = ((f32[64,8,1024]{2,1,0:T(8,128)}), f32[64,8,1024]{2,1,0:T(8,128)}, u32[]{:S(2)}, u32[]{:S(2)}) async-start(f32[64,8,1024]{2,1,0:T(8,128)} %deal.2), calls=%async_computation | async-start | bytes 4194304 | tf_op jit(solution)/shard_map/all_to_all | solution.py:567
  16.8 17.4 %copy-start.2 = (s32[28]{0:T(128)S(1)}, s32[28]{0:T(128)}, u32[]{:S(2)}) copy-start(s32[28]{0:T(128)} %owners_ref.5) | copy-start | bytes 340
  33.8 52.4 %collective-permute-start.1 = (f32[2064,256]{1,0:T(8,128)}, f32[2064,256]{1,0:T(8,128)}, u32[]{:S(2)}, u32[]{:S(2)}) collective-permute-start(f32[2064,256]{1,0:T(8,128)} %get-tuple-element.30.pack_hbm), channel_id=1, source_target_pairs={{0,32},{32,0},{64,96},{96,64},{1,33},{33,1},{65,97},{97,65},{2,34}... | collective-permute-start | bytes 6340616 | tf_op jit(solution)/shard_map/ppermute | solution.py:572
  45.4 8.3 %copy-start.3 = (s32[4]{0:T(128)S(1)}, s32[4]{0:T(128)}, u32[]{:S(2)}) copy-start(s32[4]{0:T(128)} %constant.41.clone) | copy-start | bytes 52
  45.4 8.3 %copy-start.4 = (s32[4]{0:T(128)S(1)}, s32[4]{0:T(128)}, u32[]{:S(2)}) copy-start(s32[4]{0:T(128)} %constant.40.clone) | copy-start | bytes 52
  45.4 35.7 %all-to-all-start.1 = ((f32[64,8,1024]{2,1,0:T(8,128)}), f32[64,8,1024]{2,1,0:T(8,128)S(1)}, u32[]{:S(2)}, u32[]{:S(2)}) async-start(f32[64,8,1024]{2,1,0:T(8,128)} %deal.3), calls=%async_computation.1 | async-start | bytes 4194304 | tf_op jit(solution)/shard_map/all_to_all | solution.py:567
  54.4 26.8 %copy-start.1 = (s32[6]{0:T(128)S(1)}, s32[6]{0:T(128)}, u32[]{:S(2)}) copy-start(s32[6]{0:T(128)} %pad_add_fusion.place_ref) | copy-start | bytes 76
  81.2 4.9 %copy-start = (f32[64,8,1024]{2,1,0:T(8,128)}, f32[64,8,1024]{2,1,0:T(8,128)S(1)}, u32[]{:S(2)}) copy-start(f32[64,8,1024]{2,1,0:T(8,128)S(1)} %all-to-all-done.1) | copy-start | bytes 6291460
  91.7 2.5 %collective-permute-start.2 = (f32[8,128]{1,0:T(8,128)S(1)}, f32[8,128]{1,0:T(8,128)S(1)}, u32[]{:S(2)}, u32[]{:S(2)}) collective-permute-start(f32[8,128]{1,0:T(8,128)S(1)} %get-tuple-element.34.own_ref), channel_id=1, source_target_pairs={{0,32},{32,0},{64,96},{96,64},{1,33},{33,1},{65,97},{97,65},{2,34}... | collective-permute-start | bytes 12296 | tf_op jit(solution)/shard_map/ppermute | solution.py:572
  95.9 39.0 %all-to-all-start.2 = ((f32[64,8,1024]{2,1,0:T(8,128)}), f32[64,8,1024]{2,1,0:T(8,128)S(1)}, u32[]{:S(2)}, u32[]{:S(2)}) async-start(f32[64,8,1024]{2,1,0:T(8,128)} %bitcast.9), calls=%async_computation.2 | async-start | bytes 4194304 | tf_op jit(solution)/shard_map/all_to_all | solution.py:567
